TPU v7x, 1024 devices: a whole 4x4x32 slice. The times are simulated.
1024 devices in a mesh: ens: 16 (over x, z_hi), grid: 64 (over z_lo, y, core).
Axes of the slice: x: 4, y: 4, z: 32 (z_hi: 4, z_lo: 8; z = z_hi * 8 + z_lo), core: 2. Of those that a mesh axis runs over, the one named last changes fastest.
Arguments:
- mesh_latent: bfloat16 [16, 4096, 1024], P('ens', 'grid'), may hold values from -6 to 6
- grid_latent: bfloat16 [16, 8192, 1024], P('ens', 'grid'), may hold values from -6 to 6
- edges: int32 [8192, 3], P('grid'), may hold values from 0 to 4095, as said below
- truth: float32 [100, 8192], P(None, 'grid'), may hold values from -6 to 6
- area: float32 [8192], P('grid'), may hold values from 0.3 to 3
- chan_weight: float32 [100], replicated, may hold values from 0.2 to 2
- gain: float32 [1024], replicated, may hold values from 0.5 to 1.5
- w_hidden: bfloat16 [1024, 1024], P('grid'), may hold values from -0.1875 to 0.1875
- w_out: bfloat16 [1024, 100], P('grid'), may hold values from -0.1875 to 0.1875
Outputs:
- grad_hidden: float32 [1024, 1024], P('grid')
- grad_out: float32 [1024, 100], P('grid')
- grad_gain: float32 [1024], P('grid')
- pred_grad: float32 [16, 100, 8192], P('ens', None, 'grid')
Inputs may be any that keep to these rules, and one draw needn't show every extreme that they name: `edges`: grid points 128 a block and mesh nodes 64 a block: every edge of a grid point in block b names a mesh node of block b - 1, b or b + 1, counted cyclically over the blocks.
All inputs are finite; a program needn't handle non-finite values.
Results may differ from a plain program's by a relative error of at most 0.023.
Values may be sent and summed in bfloat16 or wider, within the bound.
A program may use at most 32 MiB of HBM per device.

v0:
```python
import math

import jax
import jax.numpy as jnp
from jax import lax
from jax.sharding import PartitionSpec as P

K = 3


EPS_SMOOTH = 0.1
LN_EPS = 1e-05


def with_halo(value, sides, width):
    for axis, dim in sides:
        size, length = (lax.axis_size(axis), value.shape[dim])
        up = [(i, (i + 1) % size) for i in range(size)]
        down = [(j, i) for i, j in up]
        last = lax.slice_in_dim(value, length - width, length, axis=dim)
        leading = lax.slice_in_dim(value, 0, width, axis=dim)
        before = lax.ppermute(last, axis, up)
        after = lax.ppermute(leading, axis, down)
        value = jnp.concatenate([before, value, after], axis=dim)
    return value


def slope(diff):
    return diff / jnp.sqrt(diff * diff + EPS_SMOOTH * EPS_SMOOTH)


def gelu_tanh(value):
    return jax.nn.gelu(value, approximate=True)


def body(mesh_latent, grid_latent, edges, truth, area, chan_weight, gain, w_hidden, w_out):
    node_count = mesh_latent.shape[1]
    point_count = grid_latent.shape[1]
    members = lax.axis_size("ens")
    shards = lax.axis_size("grid")
    hidden_full, out_full = (
        lax.all_gather(w_hidden, "grid", axis=0, tiled=True),
        lax.all_gather(w_out, "grid", axis=0, tiled=True),
    )
    extended = with_halo(mesh_latent, (("grid", 1),), node_count)
    first_node = (lax.axis_index("grid") - 1) * node_count
    local_edges = (edges - first_node) % (node_count * shards)
    gathered = extended[0][local_edges]
    agg = jnp.sum(gathered.astype(jnp.float32), axis=1) / K
    state = grid_latent[0].astype(jnp.float32) + agg
    center = state - jnp.mean(state, axis=-1, keepdims=True)
    var = jnp.mean(center * center, axis=-1, keepdims=True)
    norm_hat = center * lax.rsqrt(var + LN_EPS)
    normed = (norm_hat * gain[None, :]).astype(jnp.bfloat16)
    pre = jnp.dot(normed, hidden_full, preferred_element_type=jnp.float32)
    act = gelu_tanh(pre).astype(jnp.bfloat16)
    pred = lax.dot_general(
        out_full, act, (((0,), (1,)), ((), ())), preferred_element_type=jnp.float32
    ).astype(jnp.bfloat16)
    own = pred.astype(jnp.float32)
    pair = jnp.sum(
        slope(
            own[None] - lax.all_gather(pred[None], "ens", axis=0, tiled=True).astype(jnp.float32)
        ),
        axis=0,
    )
    pred_grad = area[None, :] * chan_weight[:, None] * (slope(own - truth) - pair / (members - 1))
    grad_b = pred_grad.astype(jnp.bfloat16)
    d_act = lax.dot_general(
        grad_b, out_full, (((0,), (1,)), ((), ())), preferred_element_type=jnp.float32
    )
    d_pre = jax.vjp(gelu_tanh, pre)[1](d_act)[0].astype(jnp.bfloat16)
    scale = 1.0 / math.sqrt(members * point_count * shards)
    d_hidden = (
        lax.dot_general(normed, d_pre, (((0,), (0,)), ((), ())), preferred_element_type=jnp.float32)
        * scale
    )
    d_out = (
        lax.dot_general(act, grad_b, (((0,), (1,)), ((), ())), preferred_element_type=jnp.float32)
        * scale
    )
    d_normed = lax.dot_general(
        d_pre, hidden_full, (((1,), (1,)), ((), ())), preferred_element_type=jnp.float32
    )
    d_gain = jnp.sum(d_normed * norm_hat, axis=0) * scale
    shares = (
        lax.psum_scatter(d_hidden, "grid", scatter_dimension=0, tiled=True),
        lax.psum_scatter(d_out, "grid", scatter_dimension=0, tiled=True),
        lax.psum_scatter(d_gain, "grid", scatter_dimension=0, tiled=True),
    )
    hidden_total, out_total, gain_total = lax.psum((shares[0], shares[1], shares[2]), "ens")
    return (hidden_total, out_total, gain_total, pred_grad[None])


def solution(mesh):
    return jax.shard_map(
        body,
        mesh=mesh,
        in_specs=(
            P("ens", "grid", None),
            P("ens", "grid", None),
            P("grid", None),
            P(None, "grid"),
            P("grid"),
            P(),
            P(),
            P("grid", None),
            P("grid", None),
        ),
        out_specs=(P("grid", None), P("grid", None), P("grid"), P("ens", None, "grid")),
        check_vma=False,
    )
```

profile of v0, /device:TPU:1, one launch (start us, length us, event | category | flops | bytes accessed | tf_op | source)
XLA Modules:
  0.0 1420.1 jit_solution(16664080694140807194)
XLA Ops:
  7.2 0.7 all-gather.4.cloned.1.call-update
  7.9 4.6 collective-permute-start
  12.5 13.4 collective-permute-start.1
  26.0 0.7 compare_select_fusion
  26.6 128.7 %all_gather.10 = bf16[1024,100]{1,0:T(8,128)(2,1)} all-gather(bf16[16,100]{1,0:T(8,128)(2,1)} %param.17), channel_id=1, replica_groups=mesh['ens'=16,'grid'=64] {'grid'}, dimensions={0}, use_global_device_ids=true | all-gather | bytes 208000 | tf_op jit(solution)/shard_map/all_gather | solution.py:43
  155.3 0.1 copy.16
  155.4 0.2 reshape.29
  155.7 0.9 maximum_bitcast_fusion
  156.6 2.1 gather_fusion
  158.7 0.8 reshape.39
  159.5 1.3 reduce_sum.45
  160.8 0.2 fusion.16
  161.0 0.2 multiply_reduce_fusion
  161.2 0.1 multiply_convert_fusion.1
  161.4 2.0 fusion.17
  163.5 0.4 bitcast_convert_fusion
  163.9 77.4 %all-gather.1 = bf16[16,100,128]{2,1,0:T(8,128)(2,1)S(1)} all-gather(bf16[1,100,128]{2,1,0:T(8,128)(2,1)S(1)} %bitcast.30), channel_id=2, replica_groups=mesh['ens'=16,'grid'=64] {'ens'}, dimensions={0}, use_global_device_ids=true | all-gather | bytes 435200 | tf_op jit(solution)/shard_map/all_gather | solution.py:63
  241.3 0.2 fusion.5
  241.5 0.1 subtract_multiply_fusion
  241.6 0.5 fusion.12
  242.1 2.7 convolution_multiply_fusion
  244.8 2.4 convolution_multiply_fusion.1
  247.2 1.3 dynamic-slice
  249.2 0.8 fusion
  250.0 438.3 %reduce-scatter.3.cloned.1.call-done = f32[16,1024]{1,0:T(8,128)} async-done(((f32[1024,1024]{1,0:T(8,128)}), f32[16,1024]{1,0:T(8,128)}) %reduce-scatter.3.cloned.1.call-update) | async-done | bytes 65552 | tf_op jit(solution)/shard_map/reduce_scatter | solution.py:87
  688.3 0.7 copy.17
  689.0 218.7 %all-reduce = f32[1024]{0:T(1024)S(1)} all-reduce(f32[1024]{0:T(1024)S(1)} %broadcast_multiply_fusion), channel_id=5, replica_groups=mesh['ens'=16,'grid'=64] {'grid'}, use_global_device_ids=true, to_apply=%region_9.10.clone | all-reduce | flops 1024 | bytes 8192
  907.7 0.1 dynamic-slice.1
  907.8 223.9 %reduce-scatter.5.cloned.1.call-done = f32[16,100]{1,0:T(8,128)} async-done(((f32[1024,100]{1,0:T(8,128)}), f32[16,100]{1,0:T(8,128)}) %reduce-scatter.5.cloned.1.call-update) | async-done | bytes 6416 | tf_op jit(solution)/shard_map/reduce_scatter | solution.py:88
  1131.7 72.4 %all-reduce.1 = (f32[16,100]{1,0:T(8,128)}, f32[16]{0:T(128)}) all-reduce(f32[16,100]{1,0:T(8,128)} %reduce-scatter.5.cloned.1.call-done, f32[16]{0:T(128)S(1)} %dynamic-slice.1), channel_id=1, replica_groups=mesh['ens'=16,'grid'=64] {'ens'}, use_global_device_ids=true, to_apply=%region_7.8 | all-reduce | flops 1616 | bytes 12928 | tf_op jit(solution)/shard_map/psum | solution.py:91
  1204.1 208.0 %all-reduce.4.cloned.1.call-done = f32[16,1024]{1,0:T(8,128)} async-done(((f32[16,1024]{1,0:T(8,128)}), f32[16,1024]{1,0:T(8,128)}) %all-reduce.4.cloned.1.call-update) | async-done | bytes 65552 | tf_op jit(solution)/shard_map/psum | solution.py:91
  1412.1 1.5 copy.19
  (30 shorter events, 0.3 us)
Async XLA Ops:
  7.2 154.3 %all-gather.4.cloned.1.call-start = ((), (), s32[]{:S(2)}) async-start(), calls=%async_computation.2 | async-start | bytes 2129920 | tf_op jit(solution)/shard_map/all_gather | solution.py:42
  7.9 680.4 %reduce-scatter.3.cloned.1.call-start = ((), (), s32[]{:S(2)}) async-start(), calls=%async_computation.3 | async-start | bytes 4259840 | tf_op jit(solution)/shard_map/reduce_scatter | solution.py:87
  7.9 147.7 %collective-permute-start = (bf16[1,64,1024]{2,1,0:T(8,128)(2,1)}, bf16[1,64,1024]{2,1,0:T(8,128)(2,1)S(1)}, u32[]{:S(2)}, u32[]{:S(2)}) collective-permute-start(bf16[1,64,1024]{2,1,0:T(8,128)(2,1)} %param.9), channel_id=1, source_target_pairs={{0,1},{1,2},{2,3},{3,4},{4,5},{5,6},{6,7},{7,8},{8,9},{9,10},{10,1... | collective-permute-start | bytes 393224 | tf_op jit(solution)/shard_map/ppermute | solution.py:22
  12.5 143.1 %collective-permute-start.1 = (bf16[1,64,1024]{2,1,0:T(8,128)(2,1)}, bf16[1,64,1024]{2,1,0:T(8,128)(2,1)S(1)}, u32[]{:S(2)}, u32[]{:S(2)}) collective-permute-start(bf16[1,64,1024]{2,1,0:T(8,128)(2,1)} %param.9), channel_id=1, source_target_pairs={{1,0},{2,1},{3,2},{4,3},{5,4},{6,5},{7,6},{8,7},{9,8},{10,9},{11,1... | collective-permute-start | bytes 393224 | tf_op jit(solution)/shard_map/ppermute | solution.py:23
  159.5 1.3 copy-start.1
  159.5 1.7 copy-start.5
  161.2 2.3 copy-start.3
  161.4 80.1 %copy-start.4 = (f32[100,128]{1,0:T(8,128)S(1)}, f32[100,128]{1,0:T(8,128)}, u32[]{:S(2)}) copy-start(f32[100,128]{1,0:T(8,128)} %param.12) | copy-start | bytes 153604
  161.4 80.1 %copy-start.6 = (f32[100]{0:T(128)S(1)}, f32[100]{0:T(128)}, u32[]{:S(2)}) copy-start(f32[100]{0:T(128)} %param.14) | copy-start | bytes 1204
  161.4 80.1 %copy-start.7 = (f32[128]{0:T(128)S(1)}, f32[128]{0:T(128)}, u32[]{:S(2)}) copy-start(f32[128]{0:T(128)} %param.13) | copy-start | bytes 1540
  163.5 81.2 %copy-start.2 = (f32[128,1024]{1,0:T(8,128)}, f32[128,1024]{1,0:T(8,128)S(1)}, u32[]{:S(2)}) copy-start(f32[128,1024]{1,0:T(8,128)S(1)} %fusion.17) | copy-start | bytes 1572868
  244.7 4.4 copy-start
  244.8 886.9 %reduce-scatter.5.cloned.1.call-start = ((), (), s32[]{:S(2)}) async-start(), calls=%async_computation.5 | async-start | bytes 532480 | tf_op jit(solution)/shard_map/reduce_scatter | solution.py:88
  247.2 1164.9 %all-reduce.4.cloned.1.call-start = ((), (), s32[]{:S(2)}) async-start(), calls=%async_computation.4 | async-start | bytes 131072 | tf_op jit(solution)/shard_map/psum | solution.py:91
Sparse Core Ops, SparseCore 0:
  10.7 139.6 all-gather.3
  244.9 443.3 reduce-scatter.2
  692.0 439.6 reduce-scatter.4
  1135.0 277.0 all-reduce.3
where the time goes:
time: 1430 us; the launch traced here: 1420 us
  waiting for transfers between devices  871 us (61%)
  blocking collectives  497 us (35%)
  starting transfers between devices  18.1 us (1%)
  between operations  14.7 us (1%)
    reduce_scatter x1, waiting for transfers between devices, body(): lax.psum_scatter(d_hidden, 'grid', scatter_dimension=0, tiled=True)  438 us
    reduce_scatter x1, waiting for transfers between devices, body(): lax.psum_scatter(d_out, 'grid', scatter_dimension=0, tiled=True)  224 us
    unnamed x1, blocking collectives  219 us
    psum x1, waiting for transfers between devices, body(): lax.psum((shares[0], shares[1], shares[2]), 'ens')  208 us
    all_gather x1, blocking collectives, body(): lax.all_gather(w_out, 'grid', axis=0, tiled=True)  129 us
    all_gather x1, blocking collectives, body(): lax.all_gather(pred[None], 'ens', axis=0, tiled=True).astype(jnp.float32)  77.4 us
    psum x1, blocking collectives, body(): lax.psum((shares[0], shares[1], shares[2]), 'ens')  72.4 us
  transfers between devices with their start and end apart: 6, of which 3 were waited for; matrix products, arithmetic and copies ran while one was open for 1% of the time, Pallas kernels for 0%

commit v1 on v0

v1 whole, which is shorter than its diff:
```python
import functools
import math
from typing import NamedTuple

import jax
import jax.numpy as jnp
from jax import lax
from jax.experimental import pallas as pl
from jax.experimental.pallas import tpu as pltpu
from jax.sharding import PartitionSpec as P

LN_EPS = 1e-05
F32, BF16 = jnp.float32, jnp.bfloat16
ROWS = 16
NT = (((1,), (1,)), ((), ()))


class Sizes(NamedTuple):
    x: int = 4
    y: int = 4
    zl: int = 8
    zh: int = 4
    points: int = 128
    nodes: int = 64
    chans: int = 100
    pad: int = 128
    chunks: int = 2


def slope(diff):
    return diff * lax.rsqrt(diff * diff + 0.01)


def kernel(sz, mesh_r, grid_r, edges_r, truth_r, area_r, cw_r, gain_r, wh_r, wo_r,
           gh_o, go_o, gg_o, pg_o,
           wbuf, halo, normed, norm_t, act_t, pre, gprime, pred_s, truth_s, cw_s,
           pall, pair_s, pair_r, gb, dp_send, dp_half, dout_s,
           mb, r1, s1, s2, r2, s3f, s3, r3, ob, obf, o1, o2, o2s, o2f, r4, fin_s, fin, fo_s, fo,
           wz_s, wz_r, wy_s, wy_r, wc_s, wc_r, ha_s, ha_r, tc_s, tc_r, p1_s, p1_r, p2_s, p2_r,
           p4_s, p4_r, q1_s, q1_r, q2_s, q2_r, q3_s, q3_r, q4_s, q4_r, q5_s, q5_r, q6_s, q6_r,
           u1_s, u1_r, u2_s, u2_r):
    nx, ny, nzl, nzh = sz.x, sz.y, sz.zl, sz.zh
    nz = nzl * nzh
    hid = nzl * ny * 2 * ROWS
    slab = ny * 2 * ROWS
    half = hid // 2
    tile = half // nx
    pts, pad, nch = sz.points, sz.pad, sz.chunks
    quarter = pad // nzh
    two = 2 * ROWS
    zpc = nzl // nch

    ens, grd = lax.axis_index("ens"), lax.axis_index("grid")
    x, zh = lax.div(ens, nzh), lax.rem(ens, nzh)
    c = lax.rem(grd, 2)
    y = lax.rem(lax.div(grd, 2), ny)
    zl = lax.div(grd, 2 * ny)
    z = zh * nzl + zl
    oc = 1 - c
    ngrid = nzl * ny * 2

    def at(x_, y_, z_, c_):
        return (x_ * nzh + lax.div(z_, nzl), (lax.rem(z_, nzl) * ny + y_) * 2 + c_)

    window = []
    for d in range(1, nzl // 2 + 1):
        window.append(d)
        if d < nzl // 2 or nzl == 1:
            window.append(-d)
    window = window[: nzl - 1]

    def zdev(d):
        return at(x, y, lax.rem(z + d + nz, nz), c)

    def zhdev(i):
        return at(x, y, lax.rem(zh + i, nzh) * nzl + zl, c)

    def ydev(i):
        return at(x, lax.rem(y + i, ny), z, c)

    def xdev(i, c_):
        return at(lax.rem(x + i, nx), y, z, c_)

    left = (ens, lax.rem(grd + ngrid - 1, ngrid))
    right = (ens, lax.rem(grd + 1, ngrid))
    other = at(x, y, z, oc)

    partners = [zdev(d) for d in window] + [zdev(-d) for d in window]
    partners += [zhdev(i) for i in range(1, nzh)]
    partners += [ydev(i) for i in range(1, ny)]
    partners += [xdev(i, c) for i in range(1, nx)] + [xdev(i, oc) for i in range(1, nx)]
    partners += [left, right, other]
    barrier = pltpu.get_barrier_semaphore()
    for dev in partners:
        pl.semaphore_signal(barrier, inc=1, device_id=dev, device_id_type=pl.DeviceIdType.MESH)

    sent = []

    def copy(src, dst, ssem, rsem, dev):
        return pltpu.make_async_remote_copy(
            src_ref=src, dst_ref=dst, send_sem=ssem, recv_sem=rsem,
            device_id=dev, device_id_type=pl.DeviceIdType.MESH)

    def go(cp):
        cp.start()
        sent.append(cp)
        return cp

    wbuf[zl, y, c, :, pl.ds(0, hid)] = wh_r[...]
    wbuf[zl, y, c, :, pl.ds(hid, pad)] = jnp.zeros((ROWS, pad), BF16)
    wbuf[zl, y, c, :, pl.ds(hid, sz.chans)] = wo_r[...]
    pl.semaphore_wait(barrier, len(partners))

    offs = [0] + window
    wz = []
    for s in range(1, nzl):
        blk = wbuf.at[zl, y, c]
        wz.append(go(copy(blk, blk, wz_s.at[s], wz_r.at[s], zdev(offs[s]))))
    ha = [go(copy(mesh_r, halo.at[0], ha_s.at[0], ha_r.at[0], right)),
          go(copy(mesh_r, halo.at[1], ha_s.at[1], ha_r.at[1], left))]

    def zof(s):
        return lax.rem(zl - offs[s] + nzl, nzl)

    def wy_start(s):
        blk = wbuf.at[zof(s), y, c]
        return [go(copy(blk, blk, wy_s.at[s, i - 1], wy_r.at[s, i - 1], ydev(i)))
                for i in range(1, ny)]

    def wc_start(s):
        blk = wbuf.at[zof(s), :, c]
        return go(copy(blk, blk, wc_s.at[s], wc_r.at[s], other))

    wy, wc = {}, {}
    wy[0] = wy_start(0)

    local = (edges_r[...] - (grd - 1) * sz.nodes + ngrid * sz.nodes) % (ngrid * sz.nodes)
    lane = lax.broadcasted_iota(jnp.int32, (pts, sz.nodes), 1)

    def counts(base):
        total = jnp.zeros((pts, sz.nodes), F32)
        for k in range(3):
            total += jnp.where(local[:, k:k + 1] == lane + base, 1.0, 0.0)
        return total.astype(BF16)

    agg = jnp.dot(counts(sz.nodes), mesh_r[...], preferred_element_type=F32)
    ha[0].wait_recv()
    agg += jnp.dot(counts(0), halo[0], preferred_element_type=F32)
    ha[1].wait_recv()
    agg += jnp.dot(counts(2 * sz.nodes), halo[1], preferred_element_type=F32)
    state = grid_r[...].astype(F32) + agg / 3.0
    center = state - jnp.mean(state, axis=-1, keepdims=True)
    var = jnp.mean(center * center, axis=-1, keepdims=True)
    pre[...] = center * lax.rsqrt(var + LN_EPS) * gain_r[...]
    normed[...] = pre[...].astype(BF16)

    def turn(src, dst):
        def step(k, carry):
            cols = pl.ds(pl.multiple_of(k * slab, slab), slab)
            dst[c, cols, :] = src[:, cols].T.astype(BF16)
            return carry
        lax.fori_loop(0, nzl, step, 0)

    turn(pre, norm_t)
    tn = go(copy(norm_t.at[c], norm_t.at[c], tc_s.at[0], tc_r.at[0], other))
    pre[...] = jnp.zeros((pts, hid), F32)

    for s in range(1, nzl + 3):
        if s < nzl:
            wz[s - 1].wait_recv()
            wy[s] = wy_start(s)
        t = s - 2
        if 0 <= t < nzl:
            for cp in wy[t]:
                cp.wait_recv()
            wc[t] = wc_start(t)
        u = s - 3
        if 0 <= u < nzl:
            wc[u].wait_recv()
            zu = zof(u)
            cols = pl.ds(pl.multiple_of(zu * slab, slab), slab)
            pre[...] += jnp.dot(
                normed[:, cols], wbuf[zu, :, :, :, pl.ds(0, hid)].reshape(slab, hid),
                preferred_element_type=F32)

    k0, k1 = 0.7978845608028654, 0.044715
    v = pre[...]
    act = 0.5 * v * (1.0 + jnp.tanh(k0 * (v + k1 * v * v * v)))
    wout = wbuf[:, :, :, :, pl.ds(hid, pad)].reshape(hid, pad)
    pred_t = jnp.dot(act.astype(BF16), wout, preferred_element_type=F32)
    pred_s[...] = pred_t.T.astype(BF16).reshape(nzh, quarter, pts)
    p1 = []
    for i in range(1, nzh):
        to = lax.rem(zh + i, nzh)
        p1.append(go(copy(pred_s.at[to], pall.at[x, zh], p1_s.at[i - 1], p1_r.at[i - 1], zhdev(i))))
    pall[x, zh] = pred_s[zh]
    th = jnp.tanh(k0 * (v + k1 * v * v * v))
    gprime[...] = 0.5 * (1.0 + th) + 0.5 * v * (1.0 - th * th) * (k0 * (1.0 + 3.0 * k1 * v * v))
    pre[...] = 0.5 * v * (1.0 + th)
    turn(pre, act_t)
    ta = go(copy(act_t.at[c], act_t.at[c], tc_s.at[1], tc_r.at[1], other))
    truth_s[...] = jnp.zeros_like(truth_s)
    truth_s[pl.ds(0, sz.chans), :] = truth_r[...]
    cw_s[...] = jnp.zeros_like(cw_s)
    cw_s[pl.ds(0, 1), pl.ds(0, sz.chans)] = cw_r[...]
    weight = jnp.broadcast_to(cw_s[pl.ds(0, 1), :], (pad, pad)).T[:, 0:1] * area_r[...]
    own = pred_s[...].reshape(pad, pts).astype(F32)
    own = slope(own - truth_s[...])
    for cp in p1:
        cp.wait_recv()
    p2 = []
    for i in range(1, nx):
        p2.append(go(copy(pall.at[x], pall.at[x], p2_s.at[i - 1], p2_r.at[i - 1], xdev(i, c))))
    mine = pall[x].astype(F32)
    pair = jnp.zeros((nzh, quarter, pts), F32)
    for i in range(nx):
        if i > 0:
            p2[i - 1].wait_recv()
        src = lax.rem(x - i + nx, nx)
        for j in range(nzh):
            pair += slope(mine - pall[src, j].astype(F32)[None])
    pair_s[...] = pair.astype(BF16)
    p4 = []
    for i in range(1, nzh):
        to = lax.rem(zh + i, nzh)
        p4.append(go(copy(pair_s.at[to], pair_r.at[zh], p4_s.at[i - 1], p4_r.at[i - 1], zhdev(i))))
    pair_r[zh] = pair_s[zh]
    for cp in p4:
        cp.wait_recv()
    pgrad = weight * (own - pair_r[...].astype(F32).reshape(pad, pts) / (nx * nzh - 1.0))
    pg_o[...] = pgrad[0:sz.chans, :]
    gb[c] = pgrad.T.astype(BF16)
    tg = go(copy(gb.at[c], gb.at[c], tc_s.at[2], tc_r.at[2], other))

    def d_pre(which):
        zz = pl.ds(which * (nzl // 2), nzl // 2)
        w = wbuf[zz, :, :, :, pl.ds(hid, pad)].reshape(half, pad)
        d_act = lax.dot_general(gb[c], w, NT, preferred_element_type=F32)
        return (d_act * gprime[:, pl.ds(pl.multiple_of(which * half, half), half)]).astype(BF16)

    dp_send[...] = d_pre(oc)
    td = go(copy(dp_send, dp_half.at[c], tc_s.at[3], tc_r.at[3], other))
    dp_half[c] = d_pre(c)
    tn.wait_recv()
    td.wait_recv()

    me_a, me_b = x + (y - x) * c, y + (x - y) * c
    na = nx
    def adev(i):
        to = lax.rem(me_a + i, na)
        return to, at(to + (x - to) * c, y + (to - y) * c, z, c)

    def bdev(i):
        to = lax.rem(me_b + i, na)
        return to, at(x + (to - x) * c, to + (y - to) * c, z, c)

    q1, q2 = {}, {}
    for ch in range(nch):
        def step(k, carry):
            rows = pl.ds(pl.multiple_of((ch * zpc + k) * slab, slab), slab)
            lhs = jnp.concatenate([norm_t[0, rows, :], norm_t[1, rows, :]], axis=1)
            res = jnp.dot(lhs, dp_half[...].reshape(2 * pts, half), preferred_element_type=F32)
            res = res.astype(BF16)
            for yy in range(ny):
                for xx in range(nx):
                    a, b = xx + (yy - xx) * c, yy + (xx - yy) * c
                    mb[ch, a, b, pl.ds(pl.multiple_of(k * two, two), two), :] = (
                        res[yy * two:(yy + 1) * two, xx * tile:(xx + 1) * tile])
            return carry
        lax.fori_loop(0, zpc, step, 0)
        for i in range(1, na):
            to, dev = adev(i)
            q1[ch, i] = go(copy(mb.at[ch, to], r1.at[ch, i - 1], q1_s.at[ch, i - 1],
                                q1_r.at[ch, i - 1], dev))

    ta.wait_recv()
    tg.wait_recv()

    def out_step(k, carry):
        rows = pl.ds(pl.multiple_of(k * slab, slab), slab)
        lhs = jnp.concatenate([act_t[0, rows, :], act_t[1, rows, :]], axis=1)
        res = jnp.dot(lhs, gb[...].reshape(2 * pts, pad), preferred_element_type=F32)
        dout_s[...] = res.reshape(ny, 2, ROWS, pad)
        part = dout_s[:, c]
        obf[k] = part
        ob[k] = part.astype(BF16)
        return carry

    lax.fori_loop(0, nzl, out_step, 0)
    u1 = []
    for j, d in enumerate(window):
        to = lax.rem(zl + d + nzl, nzl)
        u1.append(go(copy(ob.at[to], o1.at[j], u1_s.at[j], u1_r.at[j], zdev(d))))

    for ch in range(nch):
        for i in range(1, na):
            q1[ch, i].wait_recv()
        total = mb[ch, me_a].astype(F32)
        for i in range(1, na):
            total += r1[ch, i - 1].astype(F32)
        s1[ch] = total
        s2[ch] = total.astype(BF16)
        for i in range(1, na):
            to, dev = bdev(i)
            q2[ch, i] = go(copy(s2.at[ch, to], r2.at[ch, i - 1], q2_s.at[ch, i - 1],
                                q2_r.at[ch, i - 1], dev))
    for cp in u1:
        cp.wait_recv()
    total = obf[zl]
    for j in range(len(window)):
        total += o1[j].astype(F32)
    o2f[...] = total
    o2s[...] = total.astype(BF16)
    u2 = []
    for i in range(1, ny):
        to = lax.rem(y + i, ny)
        u2.append(go(copy(o2s.at[to], o2.at[i - 1], u2_s.at[i - 1], u2_r.at[i - 1], ydev(i))))
    for ch in range(nch):
        for i in range(1, na):
            q2[ch, i].wait_recv()
        total = s1[ch, me_b]
        for i in range(1, na):
            total += r2[ch, i - 1].astype(F32)
        s3f[pl.ds(ch * zpc, zpc)] = total.reshape(zpc, two, tile)
        s3[pl.ds(ch * zpc, zpc)] = total.reshape(zpc, two, tile).astype(BF16)
    q3 = []
    for j, d in enumerate(window):
        to = lax.rem(zl + d + nzl, nzl)
        q3.append(go(copy(s3.at[to], r3.at[j], q3_s.at[j], q3_r.at[j], zdev(d))))
    for cp in u2:
        cp.wait_recv()
    ototal = o2f[y]
    for i in range(1, ny):
        ototal += o2[i - 1].astype(F32)
    r4[zh, pl.ds(two, ROWS), :] = ototal.astype(BF16)
    for cp in q3:
        cp.wait_recv()
    total = s3f[zl]
    for j in range(len(window)):
        total += r3[j].astype(F32)
    r4[zh, pl.ds(0, two), :] = total.astype(BF16)
    q4 = []
    for i in range(1, nzh):
        q4.append(go(copy(r4.at[zh], r4.at[zh], q4_s.at[i - 1], q4_r.at[i - 1], zhdev(i))))
    for cp in q4:
        cp.wait_recv()
    total = r4[0].astype(F32)
    for i in range(1, nzh):
        total += r4[i].astype(F32)
    fin_s[...] = total[0:two].reshape(2, ROWS, tile)
    fo[x] = total[two:two + ROWS]
    mine_t = c * nx + x
    fin[mine_t] = fin_s[c]
    q5, q6 = [], []
    q5.append(go(copy(fin_s.at[oc], fin.at[mine_t], q5_s.at[0], q5_r.at[0], other)))
    for i in range(1, nx):
        q5.append(go(copy(fin_s.at[c], fin.at[mine_t], q5_s.at[i], q5_r.at[i], xdev(i, c))))
        q5.append(go(copy(fin_s.at[oc], fin.at[mine_t], q5_s.at[nx + i - 1], q5_r.at[nx + i - 1],
                          xdev(i, oc))))
        q6.append(go(copy(fo.at[x], fo.at[x], q6_s.at[i - 1], q6_r.at[i - 1], xdev(i, c))))
    for cp in q6:
        cp.wait_recv()
    for cp in q5:
        cp.wait_recv()

    scale = 1.0 / math.sqrt(nx * nzh * pts * ngrid)
    total = fo[0]
    for i in range(1, nx):
        total += fo[i]
    go_o[...] = (total * scale)[:, 0:sz.chans]
    dots = jnp.zeros((ROWS, 1), F32)
    for t in range(2 * nx):
        part = fin[t] * scale
        gh_o[:, pl.ds(t * tile, tile)] = part
        dots += jnp.sum(part * wh_r[:, pl.ds(t * tile, tile)].astype(F32), axis=-1, keepdims=True)
    row = lax.broadcasted_iota(jnp.int32, (ROWS, hid), 0)
    col = lax.broadcasted_iota(jnp.int32, (ROWS, hid), 1)
    gains = jnp.sum(jnp.where(col == row + grd * ROWS, gain_r[...], 0.0), axis=-1, keepdims=True)
    dots = dots / gains
    row = lax.broadcasted_iota(jnp.int32, (ROWS, ROWS), 0)
    col = lax.broadcasted_iota(jnp.int32, (ROWS, ROWS), 1)
    gg_o[...] = jnp.sum(jnp.where(row == col, dots, 0.0), axis=0, keepdims=True)

    for cp in sent:
        cp.wait_send()


def body(sz, mesh_latent, grid_latent, edges, truth, area, chan_weight, gain, w_hidden, w_out):
    nx, ny, nzl, nzh = sz.x, sz.y, sz.zl, sz.zh
    hid = nzl * ny * 2 * ROWS
    half = hid // 2
    tile = half // nx
    pts, pad, nch = sz.points, sz.pad, sz.chunks
    quarter = pad // nzh
    zpc = nzl // nch
    rc = zpc * 2 * ROWS
    win = max(nzl - 1, 1)
    V = pltpu.VMEM

    def sems(*shape):
        return [pltpu.SemaphoreType.DMA(shape)] * 2

    scratch = [
        V((nzl, ny, 2, ROWS, hid + pad), BF16),
        V((2, sz.nodes, hid), BF16),
        V((pts, hid), BF16),
        V((2, hid, pts), BF16),
        V((2, hid, pts), BF16),
        V((pts, hid), F32),
        V((pts, hid), F32),
        V((nzh, quarter, pts), BF16),
        V((pad, pts), F32),
        V((8, pad), F32),
        V((nx, nzh, quarter, pts), BF16),
        V((nzh, quarter, pts), BF16),
        V((nzh, quarter, pts), BF16),
        V((2, pts, pad), BF16),
        V((pts, half), BF16),
        V((2, pts, half), BF16),
        V((ny, 2, ROWS, pad), F32),
        V((nch, nx, ny, rc, tile), BF16),
        V((nch, nx - 1, ny, rc, tile), BF16),
        V((nch, ny, rc, tile), F32),
        V((nch, ny, rc, tile), BF16),
        V((nch, ny - 1, rc, tile), BF16),
        V((nzl, 2 * ROWS, tile), F32),
        V((nzl, 2 * ROWS, tile), BF16),
        V((win, 2 * ROWS, tile), BF16),
        V((nzl, ny, ROWS, pad), BF16),
        V((nzl, ny, ROWS, pad), F32),
        V((win, ny, ROWS, pad), BF16),
        V((ny - 1, ROWS, pad), BF16),
        V((ny, ROWS, pad), BF16),
        V((ny, ROWS, pad), F32),
        V((nzh, 3 * ROWS, tile), BF16),
        V((2, ROWS, tile), F32),
        V((2 * nx, ROWS, tile), F32),
        V((8, 128), F32),
        V((nx, ROWS, pad), F32),
    ]
    scratch += sems(nzl) + sems(nzl, ny - 1) + sems(nzl) + sems(2) + sems(4)
    scratch += sems(nzh - 1) + sems(nx - 1) + sems(nzh - 1)
    scratch += sems(nch, nx - 1) + sems(nch, ny - 1) + sems(win) + sems(nzh - 1)
    scratch += sems(2 * nx - 1) + sems(nx - 1) + sems(win) + sems(ny - 1)
    vmem = pl.BlockSpec(memory_space=pltpu.VMEM)
    outs = pl.pallas_call(
        functools.partial(kernel, sz),
        out_shape=(
            jax.ShapeDtypeStruct((ROWS, hid), F32),
            jax.ShapeDtypeStruct((ROWS, sz.chans), F32),
            jax.ShapeDtypeStruct((1, ROWS), F32),
            jax.ShapeDtypeStruct((sz.chans, pts), F32),
        ),
        in_specs=[vmem] * 9,
        out_specs=(vmem,) * 4,
        scratch_shapes=scratch,
        compiler_params=pltpu.CompilerParams(
            collective_id=0, has_side_effects=True, vmem_limit_bytes=40 * 1024 * 1024),
        cost_estimate=pl.CostEstimate(flops=10**9, bytes_accessed=10**6, transcendentals=10**6),
    )(mesh_latent[0], grid_latent[0], edges, truth, area[None], chan_weight[None], gain[None],
      w_hidden, w_out)
    return outs[0], outs[1], outs[2][0], outs[3][None]


def program(mesh, sz):
    return jax.shard_map(
        functools.partial(body, sz),
        mesh=mesh,
        in_specs=(
            P("ens", "grid", None),
            P("ens", "grid", None),
            P("grid", None),
            P(None, "grid"),
            P("grid"),
            P(),
            P(),
            P("grid", None),
            P("grid", None),
        ),
        out_specs=(P("grid", None), P("grid", None), P("grid"), P("ens", None, "grid")),
        check_vma=False,
    )


def solution(mesh):
    return program(mesh, Sizes())
```

time: 1430 us -> 132 us (0.09)
  waiting for transfers between devices: 871 us -> 0 us
  blocking collectives: 497 us -> 0 us
  Pallas kernels: 0 us -> 125 us
  starting transfers between devices: 18.1 us -> 0 us
    reduce_scatter x2 -> x0, waiting for transfers between devices: 662 us -> none  [the longest x1 438 us: body(): lax.psum_scatter(d_hidden, 'grid', scatter_dimension=0, tiled=True)]
    unnamed x1 -> x0, blocking collectives: 219 us -> none
    psum x1 -> x0, waiting for transfers between devices: 208 us -> none  [body(): lax.psum((shares[0], shares[1], shares[2]), 'ens')]
    all_gather x2 -> x0, blocking collectives: 206 us -> none  [the longest x1 129 us: body(): lax.all_gather(w_out, 'grid', axis=0, tiled=True)]
    pallas_call x0 -> x1, Pallas kernels: none -> 125 us  [body(): pl.pallas_call(functools.partial(kernel, sz), out_shape=(jax.ShapeDtypeSt...]
    psum x1 -> x0, blocking collectives: 72.4 us -> none  [body(): lax.psum((shares[0], shares[1], shares[2]), 'ens')]
    ppermute x2 -> x0, starting transfers between devices: 18 us -> none  [the longest x1 13.4 us: with_halo(): after = lax.ppermute(leading, axis, down)]
  transfers between devices with their start and end apart: 6 -> 0, of which waited for: 3 -> 0; matrix products, arithmetic and copies ran while one was open for 1% -> 0% of each run, Pallas kernels for 0% -> 0%
where the time goes in v1:
time: 132 us
  Pallas kernels  125 us (95%)
  local copies, waits for them, and re-layouts  5.87 us (4%)
    pallas_call x1, Pallas kernels, body(): pl.pallas_call(functools.partial(kernel, sz), out_shape=(jax.ShapeDtypeSt...  125 us
    unnamed x21, local copies, waits for them, and re-layouts  5.87 us

profile of v1, /device:TPU:1, one launch (start us, length us, event | category | flops | bytes accessed | tf_op | source)
XLA Modules:
  0.0 131.6 jit_solution(7997538374951386645)
XLA Ops:
  0.6 0.0 copy-start.2
  0.6 0.0 copy-start.4
  0.7 0.0 copy-start.5
  0.7 0.0 copy-start.6
  0.7 0.0 copy-start.7
  0.7 0.8 copy.13.edges_r
  1.5 0.0 copy-done.2
  1.5 0.0 copy-done.4
  1.5 0.0 copy-done.5
  1.5 0.0 copy-done.6
  1.5 0.0 copy-done.7
  1.6 0.0 copy-start
  1.6 0.9 copy-done
  2.5 0.0 copy-start.1
  2.5 0.9 copy-done.1
  3.4 0.0 copy-start.3
  3.4 0.8 copy-done.3
  4.2 125.0 %shard_map.120 = (f32[16,1024]{1,0:T(8,128)S(1)}, f32[16,100]{1,0:T(8,128)S(1)}, f32[1,16]{1,0:T(1,128)S(1)}, f32[100,128]{1,0:T(8,128)S(1)}) custom-call(bf16[64,1024]{1,0:T(8,128)(2,1)S(1)} %bitcast.9, bf16[128,1024]{1,0:T(8,128)(2,1)S(1)} %bitcast.8, s32[128,3]{1,0:T(8,128)S(1)} %copy.13.edges_r, f32[100,128]{1,0:T(8,128)S(1)} %copy-done.2, ...), custom_call_target="tpu_custom_call" | custom-call | flops 1000000000 | bytes 1000000 | tf_op jit(solution)/shard_map/pallas_call | solution.py:446
  129.2 0.7 copy.14
  129.8 0.6 copy.18
  130.5 0.6 copy.19
  131.1 0.5 copy.20
Async XLA Ops:
  0.6 0.9 copy-start.2
  0.6 0.9 copy-start.4
  0.7 0.9 copy-start.5
  0.7 0.9 copy-start.6
  0.7 0.9 copy-start.7
  1.6 1.0 copy-start
  2.5 0.9 copy-start.1
  3.4 0.8 copy-start.3

commit v2 on v1

--- a/solution.py
+++ b/solution.py
@@ -24,19 +24,22 @@
     nodes: int = 64
     chans: int = 100
     pad: int = 128
-    chunks: int = 2
+    chunks: int = 4
 
 
 def slope(diff):
     return diff * lax.rsqrt(diff * diff + 0.01)
 
 
-def kernel(sz, mesh_r, grid_r, edges_r, truth_r, area_r, cw_r, gain_r, wh_r, wo_r,
+def kernel(sz, mesh_h, grid_h, edges_h, truth_h, area_h, cw_h, gain_h, wh_h, wo_h,
            gh_o, go_o, gg_o, pg_o,
+           mesh_r, grid_r, edges_r, truth_r, area_r, cw_r, gain_r, wo_r,
            wbuf, halo, normed, norm_t, act_t, pre, gprime, pred_s, truth_s, cw_s,
            pall, pair_s, pair_r, gb, dp_send, dp_half, dout_s,
-           mb, r1, s1, s2, r2, s3f, s3, r3, ob, obf, o1, o2, o2s, o2f, r4, fin_s, fin, fo_s, fo,
-           wz_s, wz_r, wy_s, wy_r, wc_s, wc_r, ha_s, ha_r, tc_s, tc_r, p1_s, p1_r, p2_s, p2_r,
+           mb, r1, s1, s2, r2, s3, r3, ob, obf, o1, o2, o2s, o2f, r4, fin_s, fin, fo,
+           near, far, lo_s,
+           wz_s, wz_r, wy_s, wy_r, wx_s, wx_r, wc_s, wc_r, ha_s, ha_r, tc_s, tc_r,
+           p1_s, p1_r, p2_s, p2_r,
            p4_s, p4_r, q1_s, q1_r, q2_s, q2_r, q3_s, q3_r, q4_s, q4_r, q5_s, q5_r, q6_s, q6_r,
            u1_s, u1_r, u2_s, u2_r):
     nx, ny, nzl, nzh = sz.x, sz.y, sz.zl, sz.zh
@@ -46,7 +49,7 @@
     half = hid // 2
     tile = half // nx
     pts, pad, nch = sz.points, sz.pad, sz.chunks
-    quarter = pad // nzh
+    quarter = pad // nx
     two = 2 * ROWS
     zpc = nzl // nch
 
@@ -85,14 +88,25 @@
     right = (ens, lax.rem(grd + 1, ngrid))
     other = at(x, y, z, oc)
 
+    def signal(sem, dev):
+        pl.semaphore_signal(sem, inc=1, device_id=dev, device_id_type=pl.DeviceIdType.MESH)
+
     partners = [zdev(d) for d in window] + [zdev(-d) for d in window]
-    partners += [zhdev(i) for i in range(1, nzh)]
     partners += [ydev(i) for i in range(1, ny)]
     partners += [xdev(i, c) for i in range(1, nx)] + [xdev(i, oc) for i in range(1, nx)]
     partners += [left, right, other]
     barrier = pltpu.get_barrier_semaphore()
     for dev in partners:
-        pl.semaphore_signal(barrier, inc=1, device_id=dev, device_id_type=pl.DeviceIdType.MESH)
+        signal(barrier, dev)
+
+    def fetch(k, src, dst):
+        cp = pltpu.make_async_copy(src, dst, lo_s.at[k])
+        cp.start()
+        return cp
+
+    lo_m = [fetch(2, mesh_h, mesh_r), fetch(3, edges_h, edges_r), fetch(4, grid_h, grid_r),
+            fetch(5, gain_h, gain_r)]
+    lo_t = [fetch(6, truth_h, truth_r), fetch(7, area_h, area_r), fetch(8, cw_h, cw_r)]
 
     sent = []
 
@@ -106,44 +120,73 @@
         sent.append(cp)
         return cp
 
-    wbuf[zl, y, c, :, pl.ds(0, hid)] = wh_r[...]
-    wbuf[zl, y, c, :, pl.ds(hid, pad)] = jnp.zeros((ROWS, pad), BF16)
-    wbuf[zl, y, c, :, pl.ds(hid, sz.chans)] = wo_r[...]
+    odd = lax.rem(zl, 2)
+    zb = 2 * x + 1
+    spread = jnp.logical_or(odd == 0, zl == zb)
+
+    @pl.when(spread)
+    def _():
+        wbuf[zl, y, c, :, pl.ds(hid, pad)] = jnp.zeros((ROWS, pad), BF16)
+        lo_w = [fetch(0, wh_h, wbuf.at[zl, y, c, :, pl.ds(0, hid)]), fetch(1, wo_h, wo_r)]
+        for cp in lo_w:
+            cp.wait()
+        wbuf[zl, y, c, :, pl.ds(hid, sz.chans)] = wo_r[...]
+
     pl.semaphore_wait(barrier, len(partners))
 
-    offs = [0] + window
-    wz = []
-    for s in range(1, nzl):
-        blk = wbuf.at[zl, y, c]
-        wz.append(go(copy(blk, blk, wz_s.at[s], wz_r.at[s], zdev(offs[s]))))
-    ha = [go(copy(mesh_r, halo.at[0], ha_s.at[0], ha_r.at[0], right)),
-          go(copy(mesh_r, halo.at[1], ha_s.at[1], ha_r.at[1], left))]
-
-    def zof(s):
-        return lax.rem(zl - offs[s] + nzl, nzl)
-
-    def wy_start(s):
-        blk = wbuf.at[zof(s), y, c]
-        return [go(copy(blk, blk, wy_s.at[s, i - 1], wy_r.at[s, i - 1], ydev(i)))
+    reach = nzl // 2
+    signal(near, zdev(reach))
+    signal(near, zdev(-reach))
+
+    block = wbuf.at[zl, y, c]
+    wz = {d: copy(block, block, wz_s.at[j], wz_r.at[zl], zdev(d)) for j, d in enumerate(window)}
+
+    @pl.when(spread)
+    def _():
+        for d in window:
+            wz[d].start()
+
+    def wz_wait(zk):
+        got = wbuf.at[zk, y, c]
+        copy(got, got, wz_s.at[0], wz_r.at[zk], zdev(1)).wait_recv()
+
+    def wy_start(zk):
+        blk = wbuf.at[zk, y, c]
+        return [go(copy(blk, blk, wy_s.at[zk, i - 1], wy_r.at[zk, i - 1], ydev(i)))
                 for i in range(1, ny)]
 
-    def wc_start(s):
-        blk = wbuf.at[zof(s), :, c]
-        return go(copy(blk, blk, wc_s.at[s], wc_r.at[s], other))
-
-    wy, wc = {}, {}
-    wy[0] = wy_start(0)
-
+    def wc_start(zk):
+        blk = wbuf.at[zk, :, c]
+        return go(copy(blk, blk, wc_s.at[zk], wc_r.at[zk], other))
+
+    evens = [0] + [-d for d in window if d % 2 == 0]
+    odds = [-d for d in window if d % 2 == 1]
+    za = [lax.rem(zl + e + (o - e) * odd + nzl, nzl) for e, o in zip(evens, odds, strict=True)]
+    nk = len(za)
+    wy = {}
+
+    @pl.when(odd == 1)
+    def _():
+        wz_wait(za[0])
+    wy[0] = wy_start(za[0])
+    ha = [go(copy(mesh_h, halo.at[0], ha_s.at[0], ha_r.at[0], right)),
+          go(copy(mesh_h, halo.at[1], ha_s.at[1], ha_r.at[1], left))]
+
+    for cp in lo_m:
+        cp.wait()
     local = (edges_r[...] - (grd - 1) * sz.nodes + ngrid * sz.nodes) % (ngrid * sz.nodes)
-    lane = lax.broadcasted_iota(jnp.int32, (pts, sz.nodes), 1)
+    node = lax.broadcasted_iota(jnp.int32, (sz.nodes, pts), 0)
 
     def counts(base):
-        total = jnp.zeros((pts, sz.nodes), F32)
+        total = jnp.zeros((sz.nodes, pts), F32)
         for k in range(3):
-            total += jnp.where(local[:, k:k + 1] == lane + base, 1.0, 0.0)
-        return total.astype(BF16)
+            total += jnp.where(local[k:k + 1, :] == node + base, 1.0, 0.0)
+        return total.T.astype(BF16)
 
     agg = jnp.dot(counts(sz.nodes), mesh_r[...], preferred_element_type=F32)
+    for k in range(1, nk - 1):
+        wz_wait(za[k])
+        wy[k] = wy_start(za[k])
     ha[0].wait_recv()
     agg += jnp.dot(counts(0), halo[0], preferred_element_type=F32)
     ha[1].wait_recv()
@@ -165,40 +208,76 @@
     tn = go(copy(norm_t.at[c], norm_t.at[c], tc_s.at[0], tc_r.at[0], other))
     pre[...] = jnp.zeros((pts, hid), F32)
 
-    for s in range(1, nzl + 3):
-        if s < nzl:
-            wz[s - 1].wait_recv()
-            wy[s] = wy_start(s)
-        t = s - 2
-        if 0 <= t < nzl:
-            for cp in wy[t]:
-                cp.wait_recv()
-            wc[t] = wc_start(t)
-        u = s - 3
-        if 0 <= u < nzl:
-            wc[u].wait_recv()
-            zu = zof(u)
-            cols = pl.ds(pl.multiple_of(zu * slab, slab), slab)
-            pre[...] += jnp.dot(
-                normed[:, cols], wbuf[zu, :, :, :, pl.ds(0, hid)].reshape(slab, hid),
-                preferred_element_type=F32)
+    @pl.when(zl != zb)
+    def _():
+        wz_wait(zb)
+    wyb = wy_start(zb)
+    if nk > 1:
+        wz_wait(za[nk - 1])
+        wy[nk - 1] = wy_start(za[nk - 1])
+
+    def slab_in(k):
+        for cp in wy[k]:
+            cp.wait_recv()
+        wc_start(za[k])
+
+    def multiply(zk):
+        got = wbuf.at[zk, :, oc]
+        copy(got, got, wc_s.at[zk], wc_r.at[zk], other).wait_recv()
+        cols = pl.ds(pl.multiple_of(zk * slab, slab), slab)
+        pre[...] += jnp.dot(
+            normed[:, cols], wbuf[zk, :, :, :, pl.ds(0, hid)].reshape(slab, hid),
+            preferred_element_type=F32)
+
+    slab_in(0)
+    for cp in wyb:
+        cp.wait_recv()
+    wx = []
+    for i in range(1, nx):
+        blk = wbuf.at[zb, :, c]
+        wx.append(go(copy(blk, blk, wx_s.at[i - 1], wx_r.at[i - 1], xdev(i, c))))
+    wc_start(zb)
+    pl.semaphore_wait(near, 2)
+    signal(far, zhdev(1))
+    signal(far, zhdev(nzh - 1))
+    for k in range(1, nk):
+        slab_in(k)
+        multiply(za[k - 1])
+    multiply(zb)
+    zx = [2 * lax.rem(x - i + nx, nx) + 1 for i in range(nx)]
+    order = [1] + ([nx - 1] if nx > 2 else []) + list(range(2, nx - 1))
+    for k, i in enumerate(order):
+        got = wbuf.at[zx[i], :, c]
+        copy(got, got, wx_s.at[i - 1], wx_r.at[i - 1], xdev(i, c)).wait_recv()
+        wc_start(zx[i])
+        multiply(za[nk - 1] if k == 0 else zx[order[k - 1]])
+    multiply(zx[order[-1]])
 
     k0, k1 = 0.7978845608028654, 0.044715
     v = pre[...]
     act = 0.5 * v * (1.0 + jnp.tanh(k0 * (v + k1 * v * v * v)))
     wout = wbuf[:, :, :, :, pl.ds(hid, pad)].reshape(hid, pad)
     pred_t = jnp.dot(act.astype(BF16), wout, preferred_element_type=F32)
-    pred_s[...] = pred_t.T.astype(BF16).reshape(nzh, quarter, pts)
+    pred_s[...] = pred_t.T.astype(BF16).reshape(nx, quarter, pts)
     p1 = []
-    for i in range(1, nzh):
-        to = lax.rem(zh + i, nzh)
-        p1.append(go(copy(pred_s.at[to], pall.at[x, zh], p1_s.at[i - 1], p1_r.at[i - 1], zhdev(i))))
-    pall[x, zh] = pred_s[zh]
+    for i in range(1, nx):
+        to = lax.rem(x + i, nx)
+        p1.append(go(copy(pred_s.at[to], pall.at[zh, x], p1_s.at[i - 1], p1_r.at[i - 1], xdev(i, c))))
+    pall[zh, x] = pred_s[x]
+    pl.semaphore_wait(far, 2)
+    for cp in p1:
+        cp.wait_recv()
+    zorder = [nzh // 2] + [i for i in range(1, nzh) if i != nzh // 2]
+    p2 = {}
+    for i in zorder:
+        p2[i] = go(copy(pall.at[zh], pall.at[zh], p2_s.at[i - 1], p2_r.at[i - 1], zhdev(i)))
     th = jnp.tanh(k0 * (v + k1 * v * v * v))
     gprime[...] = 0.5 * (1.0 + th) + 0.5 * v * (1.0 - th * th) * (k0 * (1.0 + 3.0 * k1 * v * v))
     pre[...] = 0.5 * v * (1.0 + th)
     turn(pre, act_t)
     ta = go(copy(act_t.at[c], act_t.at[c], tc_s.at[1], tc_r.at[1], other))
+    for cp in lo_t:
+        cp.wait()
     truth_s[...] = jnp.zeros_like(truth_s)
     truth_s[pl.ds(0, sz.chans), :] = truth_r[...]
     cw_s[...] = jnp.zeros_like(cw_s)
@@ -206,25 +285,20 @@
     weight = jnp.broadcast_to(cw_s[pl.ds(0, 1), :], (pad, pad)).T[:, 0:1] * area_r[...]
     own = pred_s[...].reshape(pad, pts).astype(F32)
     own = slope(own - truth_s[...])
-    for cp in p1:
-        cp.wait_recv()
-    p2 = []
-    for i in range(1, nx):
-        p2.append(go(copy(pall.at[x], pall.at[x], p2_s.at[i - 1], p2_r.at[i - 1], xdev(i, c))))
-    mine = pall[x].astype(F32)
-    pair = jnp.zeros((nzh, quarter, pts), F32)
-    for i in range(nx):
+    mine = pall[zh].astype(F32)
+    pair = jnp.zeros((nx, quarter, pts), F32)
+    for i in [0] + zorder[1:] + zorder[:1]:
         if i > 0:
-            p2[i - 1].wait_recv()
-        src = lax.rem(x - i + nx, nx)
-        for j in range(nzh):
+            p2[i].wait_recv()
+        src = lax.rem(zh - i + nzh, nzh)
+        for j in range(nx):
             pair += slope(mine - pall[src, j].astype(F32)[None])
     pair_s[...] = pair.astype(BF16)
     p4 = []
-    for i in range(1, nzh):
-        to = lax.rem(zh + i, nzh)
-        p4.append(go(copy(pair_s.at[to], pair_r.at[zh], p4_s.at[i - 1], p4_r.at[i - 1], zhdev(i))))
-    pair_r[zh] = pair_s[zh]
+    for i in range(1, nx):
+        to = lax.rem(x + i, nx)
+        p4.append(go(copy(pair_s.at[to], pair_r.at[x], p4_s.at[i - 1], p4_r.at[i - 1], xdev(i, c))))
+    pair_r[x] = pair_s[x]
     for cp in p4:
         cp.wait_recv()
     pgrad = weight * (own - pair_r[...].astype(F32).reshape(pad, pts) / (nx * nzh - 1.0))
@@ -315,32 +389,38 @@
     for i in range(1, ny):
         to = lax.rem(y + i, ny)
         u2.append(go(copy(o2s.at[to], o2.at[i - 1], u2_s.at[i - 1], u2_r.at[i - 1], ydev(i))))
+    q3 = {}
     for ch in range(nch):
         for i in range(1, na):
             q2[ch, i].wait_recv()
         total = s1[ch, me_b]
         for i in range(1, na):
             total += r2[ch, i - 1].astype(F32)
-        s3f[pl.ds(ch * zpc, zpc)] = total.reshape(zpc, two, tile)
         s3[pl.ds(ch * zpc, zpc)] = total.reshape(zpc, two, tile).astype(BF16)
-    q3 = []
-    for j, d in enumerate(window):
-        to = lax.rem(zl + d + nzl, nzl)
-        q3.append(go(copy(s3.at[to], r3.at[j], q3_s.at[j], q3_r.at[j], zdev(d))))
+        for zt in range(ch * zpc, (ch + 1) * zpc):
+            d = lax.rem(zt - zl + 2 * nzl - 1 - nzl // 2, nzl) - (nzl // 2 - 1)
+            q3[zt] = copy(s3.at[zt], r3.at[zl], q3_s.at[zt], q3_r.at[zl], zdev(d))
+
+            @pl.when(zl != zt)
+            def _(zt=zt):
+                q3[zt].start()
+    r3[zl] = s3[zl]
     for cp in u2:
         cp.wait_recv()
     ototal = o2f[y]
     for i in range(1, ny):
         ototal += o2[i - 1].astype(F32)
     r4[zh, pl.ds(two, ROWS), :] = ototal.astype(BF16)
-    for cp in q3:
-        cp.wait_recv()
-    total = s3f[zl]
-    for j in range(len(window)):
-        total += r3[j].astype(F32)
+    for k in range(nzl):
+        @pl.when(zl != k)
+        def _(k=k):
+            copy(s3.at[k], r3.at[k], q3_s.at[k], q3_r.at[k], zdev(1)).wait_recv()
+    total = r3[0].astype(F32)
+    for k in range(1, nzl):
+        total += r3[k].astype(F32)
     r4[zh, pl.ds(0, two), :] = total.astype(BF16)
     q4 = []
-    for i in range(1, nzh):
+    for i in zorder:
         q4.append(go(copy(r4.at[zh], r4.at[zh], q4_s.at[i - 1], q4_r.at[i - 1], zhdev(i))))
     for cp in q4:
         cp.wait_recv()
@@ -372,7 +452,7 @@
     for t in range(2 * nx):
         part = fin[t] * scale
         gh_o[:, pl.ds(t * tile, tile)] = part
-        dots += jnp.sum(part * wh_r[:, pl.ds(t * tile, tile)].astype(F32), axis=-1, keepdims=True)
+        dots += jnp.sum(part * wbuf[zl, y, c, :, pl.ds(t * tile, tile)].astype(F32), axis=-1, keepdims=True)
     row = lax.broadcasted_iota(jnp.int32, (ROWS, hid), 0)
     col = lax.broadcasted_iota(jnp.int32, (ROWS, hid), 1)
     gains = jnp.sum(jnp.where(col == row + grd * ROWS, gain_r[...], 0.0), axis=-1, keepdims=True)
@@ -384,6 +464,15 @@
     for cp in sent:
         cp.wait_send()
 
+    @pl.when(spread)
+    def _():
+        for d in window:
+            wz[d].wait_send()
+    for zt in range(nzl):
+        @pl.when(zl != zt)
+        def _(zt=zt):
+            q3[zt].wait_send()
+
 
 def body(sz, mesh_latent, grid_latent, edges, truth, area, chan_weight, gain, w_hidden, w_out):
     nx, ny, nzl, nzh = sz.x, sz.y, sz.zl, sz.zh
@@ -391,7 +480,7 @@
     half = hid // 2
     tile = half // nx
     pts, pad, nch = sz.points, sz.pad, sz.chunks
-    quarter = pad // nzh
+    quarter = pad // nx
     zpc = nzl // nch
     rc = zpc * 2 * ROWS
     win = max(nzl - 1, 1)
@@ -401,6 +490,14 @@
         return [pltpu.SemaphoreType.DMA(shape)] * 2
 
     scratch = [
+        V((sz.nodes, hid), BF16),
+        V((pts, hid), BF16),
+        V((3, pts), jnp.int32),
+        V((sz.chans, pts), F32),
+        V((1, pts), F32),
+        V((1, sz.chans), F32),
+        V((1, hid), F32),
+        V((ROWS, sz.chans), BF16),
         V((nzl, ny, 2, ROWS, hid + pad), BF16),
         V((2, sz.nodes, hid), BF16),
         V((pts, hid), BF16),
@@ -408,12 +505,12 @@
         V((2, hid, pts), BF16),
         V((pts, hid), F32),
         V((pts, hid), F32),
-        V((nzh, quarter, pts), BF16),
+        V((nx, quarter, pts), BF16),
         V((pad, pts), F32),
         V((8, pad), F32),
-        V((nx, nzh, quarter, pts), BF16),
-        V((nzh, quarter, pts), BF16),
-        V((nzh, quarter, pts), BF16),
+        V((nzh, nx, quarter, pts), BF16),
+        V((nx, quarter, pts), BF16),
+        V((nx, quarter, pts), BF16),
         V((2, pts, pad), BF16),
         V((pts, half), BF16),
         V((2, pts, half), BF16),
@@ -423,9 +520,8 @@
         V((nch, ny, rc, tile), F32),
         V((nch, ny, rc, tile), BF16),
         V((nch, ny - 1, rc, tile), BF16),
-        V((nzl, 2 * ROWS, tile), F32),
         V((nzl, 2 * ROWS, tile), BF16),
-        V((win, 2 * ROWS, tile), BF16),
+        V((nzl, 2 * ROWS, tile), BF16),
         V((nzl, ny, ROWS, pad), BF16),
         V((nzl, ny, ROWS, pad), F32),
         V((win, ny, ROWS, pad), BF16),
@@ -435,12 +531,14 @@
         V((nzh, 3 * ROWS, tile), BF16),
         V((2, ROWS, tile), F32),
         V((2 * nx, ROWS, tile), F32),
-        V((8, 128), F32),
         V((nx, ROWS, pad), F32),
+        pltpu.SemaphoreType.REGULAR,
+        pltpu.SemaphoreType.REGULAR,
+        pltpu.SemaphoreType.DMA((9,)),
     ]
-    scratch += sems(nzl) + sems(nzl, ny - 1) + sems(nzl) + sems(2) + sems(4)
-    scratch += sems(nzh - 1) + sems(nx - 1) + sems(nzh - 1)
-    scratch += sems(nch, nx - 1) + sems(nch, ny - 1) + sems(win) + sems(nzh - 1)
+    scratch += sems(nzl) + sems(nzl, ny - 1) + sems(nx - 1) + sems(nzl) + sems(2) + sems(4)
+    scratch += sems(nx - 1) + sems(nzh - 1) + sems(nx - 1)
+    scratch += sems(nch, nx - 1) + sems(nch, ny - 1) + sems(nzl) + sems(nzh - 1)
     scratch += sems(2 * nx - 1) + sems(nx - 1) + sems(win) + sems(ny - 1)
     vmem = pl.BlockSpec(memory_space=pltpu.VMEM)
     outs = pl.pallas_call(
@@ -451,14 +549,15 @@
             jax.ShapeDtypeStruct((1, ROWS), F32),
             jax.ShapeDtypeStruct((sz.chans, pts), F32),
         ),
-        in_specs=[vmem] * 9,
+        in_specs=[pl.BlockSpec(memory_space=pltpu.HBM)] * 9,
         out_specs=(vmem,) * 4,
         scratch_shapes=scratch,
         compiler_params=pltpu.CompilerParams(
             collective_id=0, has_side_effects=True, vmem_limit_bytes=40 * 1024 * 1024),
         cost_estimate=pl.CostEstimate(flops=10**9, bytes_accessed=10**6, transcendentals=10**6),
-    )(mesh_latent[0], grid_latent[0], edges, truth, area[None], chan_weight[None], gain[None],
-      w_hidden, w_out)
+    )(*[pltpu.with_memory_space_constraint(a, pltpu.HBM) for a in (
+        mesh_latent[0], grid_latent[0], edges.T, truth, area[None], chan_weight[None], gain[None],
+        w_hidden, w_out)])
     return outs[0], outs[1], outs[2][0], outs[3][None]
 
 

time: 132 us -> 112 us (0.85)
  Pallas kernels: 125 us -> 109 us
  local copies, waits for them, and re-layouts: 5.87 us -> 2.41 us
    pallas_call x1, Pallas kernels: 125 us -> 109 us  [body(): pl.pallas_call(functools.partial(kernel, sz), out_shape=(jax.ShapeDtypeSt...]
    unnamed x21 -> x4, local copies, waits for them, and re-layouts: 5.87 us -> 2.41 us
where the time goes in v2:
time: 112 us
  Pallas kernels  109 us (97%)
  local copies, waits for them, and re-layouts  2.41 us (2%)
    pallas_call x1, Pallas kernels, body(): pl.pallas_call(functools.partial(kernel, sz), out_shape=(jax.ShapeDtypeSt...  109 us
    unnamed x4, local copies, waits for them, and re-layouts  2.41 us

profile of v2, /device:TPU:1, one launch (start us, length us, event | category | flops | bytes accessed | tf_op | source)
XLA Modules:
  0.0 111.8 jit_solution(15007255703248979831)
XLA Ops:
  0.6 108.7 %shard_map.120 = (f32[16,1024]{1,0:T(8,128)S(1)}, f32[16,100]{1,0:T(8,128)S(1)}, f32[1,16]{1,0:T(1,128)S(1)}, f32[100,128]{1,0:T(8,128)S(1)}) custom-call(bf16[64,1024]{1,0:T(8,128)(2,1)} %bitcast.11, bf16[128,1024]{1,0:T(8,128)(2,1)} %bitcast.10, s32[3,128]{1,0:T(4,128)} %bitcast.13, f32[100,128]{1,0:T(8,128)} %truth_h.1, f32[1,128]{1,0:T(1,128)} %bitcast.14, ...), custom_call_target="tpu_custom_call" | custom-call | flops 1000000000 | bytes 1000000 | tf_op jit(solution)/shard_map/pallas_call | solution.py:544
  109.4 0.7 copy.13
  110.0 0.6 copy.17
  110.7 0.6 copy.18
  111.3 0.5 copy.19

commit v3 on v2

--- a/solution.py
+++ b/solution.py
@@ -34,13 +34,14 @@
 def kernel(sz, mesh_h, grid_h, edges_h, truth_h, area_h, cw_h, gain_h, wh_h, wo_h,
            gh_o, go_o, gg_o, pg_o,
            mesh_r, grid_r, edges_r, truth_r, area_r, cw_r, gain_r, wo_r,
-           wbuf, halo, normed, norm_t, act_t, pre, gprime, pred_s, truth_s, cw_s,
-           pall, pair_s, pair_r, gb, dp_send, dp_half, dout_s,
-           mb, r1, s1, s2, r2, s3, r3, ob, obf, o1, o2, o2s, o2f, r4, fin_s, fin, fo,
+           wbuf, halo, normed, norm_t, act_t, pre, gprime, truth_s, cw_s,
+           pall, gb, dp_send, dp_all, dout_s,
+           mb, r2, s3, r3, ob, obf, o1, o2, o2s, o2f, r4, fin_s, fin, fo,
            near, far, lo_s,
+           xn_s, xn_r, cn_s, cn_r,
            wz_s, wz_r, wy_s, wy_r, wx_s, wx_r, wc_s, wc_r, ha_s, ha_r, tc_s, tc_r,
            p1_s, p1_r, p2_s, p2_r,
-           p4_s, p4_r, q1_s, q1_r, q2_s, q2_r, q3_s, q3_r, q4_s, q4_r, q5_s, q5_r, q6_s, q6_r,
+           q1_s, q1_r, q2_s, q2_r, q3_s, q3_r, q4_s, q4_r, q5_s, q5_r, q6_s, q6_r,
            u1_s, u1_r, u2_s, u2_r):
     nx, ny, nzl, nzh = sz.x, sz.y, sz.zl, sz.zh
     nz = nzl * nzh
@@ -49,7 +50,7 @@
     half = hid // 2
     tile = half // nx
     pts, pad, nch = sz.points, sz.pad, sz.chunks
-    quarter = pad // nx
+    sent_rows = -(-sz.chans // ROWS) * ROWS
     two = 2 * ROWS
     zpc = nzl // nch
 
@@ -169,8 +170,6 @@
     def _():
         wz_wait(za[0])
     wy[0] = wy_start(za[0])
-    ha = [go(copy(mesh_h, halo.at[0], ha_s.at[0], ha_r.at[0], right)),
-          go(copy(mesh_h, halo.at[1], ha_s.at[1], ha_r.at[1], left))]
 
     for cp in lo_m:
         cp.wait()
@@ -184,9 +183,38 @@
         return total.T.astype(BF16)
 
     agg = jnp.dot(counts(sz.nodes), mesh_r[...], preferred_element_type=F32)
-    for k in range(1, nk - 1):
+
+    def wx_start(j):
+        blk = wbuf.at[zb, lax.rem(y - j + ny, ny), c]
+        for i in range(1, nx):
+            go(copy(blk, blk, wx_s.at[i - 1, j], wx_r.at[i - 1, j], xdev(i, c)))
+
+    ha = [go(copy(mesh_h, halo.at[0], ha_s.at[0], ha_r.at[0], right)),
+          go(copy(mesh_h, halo.at[1], ha_s.at[1], ha_r.at[1], left))]
+
+    @pl.when(zl != zb)
+    def _():
+        wz_wait(zb)
+    wyb = wy_start(zb)
+    wx_start(0)
+    for k in range(1, nk):
         wz_wait(za[k])
         wy[k] = wy_start(za[k])
+    for j in range(1, ny):
+        wyb[j - 1].wait_recv()
+        wx_start(j)
+    wc_start(zb)
+    pl.semaphore_wait(near, 2)
+    signal(far, zhdev(1))
+    signal(far, zhdev(nzh - 1))
+
+    def slab_in(k):
+        for cp in wy[k]:
+            cp.wait_recv()
+        wc_start(za[k])
+
+    slab_in(0)
+
     ha[0].wait_recv()
     agg += jnp.dot(counts(0), halo[0], preferred_element_type=F32)
     ha[1].wait_recv()
@@ -200,26 +228,11 @@
     def turn(src, dst):
         def step(k, carry):
             cols = pl.ds(pl.multiple_of(k * slab, slab), slab)
-            dst[c, cols, :] = src[:, cols].T.astype(BF16)
+            dst[cols, :] = src[:, cols].astype(F32).T.astype(BF16)
             return carry
         lax.fori_loop(0, nzl, step, 0)
 
-    turn(pre, norm_t)
-    tn = go(copy(norm_t.at[c], norm_t.at[c], tc_s.at[0], tc_r.at[0], other))
     pre[...] = jnp.zeros((pts, hid), F32)
-
-    @pl.when(zl != zb)
-    def _():
-        wz_wait(zb)
-    wyb = wy_start(zb)
-    if nk > 1:
-        wz_wait(za[nk - 1])
-        wy[nk - 1] = wy_start(za[nk - 1])
-
-    def slab_in(k):
-        for cp in wy[k]:
-            cp.wait_recv()
-        wc_start(za[k])
 
     def multiply(zk):
         got = wbuf.at[zk, :, oc]
@@ -229,53 +242,55 @@
             normed[:, cols], wbuf[zk, :, :, :, pl.ds(0, hid)].reshape(slab, hid),
             preferred_element_type=F32)
 
-    slab_in(0)
-    for cp in wyb:
-        cp.wait_recv()
-    wx = []
-    for i in range(1, nx):
-        blk = wbuf.at[zb, :, c]
-        wx.append(go(copy(blk, blk, wx_s.at[i - 1], wx_r.at[i - 1], xdev(i, c))))
-    wc_start(zb)
-    pl.semaphore_wait(near, 2)
-    signal(far, zhdev(1))
-    signal(far, zhdev(nzh - 1))
     for k in range(1, nk):
         slab_in(k)
-        multiply(za[k - 1])
-    multiply(zb)
+    ready = za[:1] + [zb] + za[1:]
+    multiply(ready.pop(0))
+    multiply(ready.pop(0))
     zx = [2 * lax.rem(x - i + nx, nx) + 1 for i in range(nx)]
     order = [1] + ([nx - 1] if nx > 2 else []) + list(range(2, nx - 1))
     for k, i in enumerate(order):
-        got = wbuf.at[zx[i], :, c]
-        copy(got, got, wx_s.at[i - 1], wx_r.at[i - 1], xdev(i, c)).wait_recv()
+        for j in range(ny):
+            got = wbuf.at[zx[i], lax.rem(y - j + ny, ny), c]
+            copy(got, got, wx_s.at[i - 1, j], wx_r.at[i - 1, j], xdev(i, c)).wait_recv()
         wc_start(zx[i])
-        multiply(za[nk - 1] if k == 0 else zx[order[k - 1]])
-    multiply(zx[order[-1]])
+        multiply(ready.pop(0))
+        ready.append(zx[i])
+    for zk in ready:
+        multiply(zk)
 
     k0, k1 = 0.7978845608028654, 0.044715
     v = pre[...]
     act = 0.5 * v * (1.0 + jnp.tanh(k0 * (v + k1 * v * v * v)))
     wout = wbuf[:, :, :, :, pl.ds(hid, pad)].reshape(hid, pad)
     pred_t = jnp.dot(act.astype(BF16), wout, preferred_element_type=F32)
-    pred_s[...] = pred_t.T.astype(BF16).reshape(nx, quarter, pts)
-    p1 = []
+    send = pl.ds(0, sent_rows)
+    pall[zh, x] = pred_t.T.astype(BF16)
+    pl.semaphore_wait(far, 2)
+    zorder = [nzh // 2] + [i for i in range(1, nzh) if i != nzh // 2]
+    xorder = [nx // 2] + [i for i in range(1, nx) if i != nx // 2]
+    p1, p2 = {}, {}
+    for i in zorder:
+        blk = pall.at[zh, x, send]
+        p1[i] = go(copy(blk, blk, p1_s.at[i - 1], p1_r.at[i - 1], zhdev(i)))
+
+    def share(i):
+        blk = pall.at[lax.rem(zh - i + nzh, nzh), x, send]
+        for j in xorder:
+            p2[i, j] = go(copy(blk, blk, p2_s.at[i, j - 1], p2_r.at[i, j - 1], xdev(j, c)))
+
+    share(0)
+    me = x * 2 + c
+    turn(normed, norm_t.at[me])
+    cn = [go(copy(norm_t.at[me], norm_t.at[me], cn_s.at[0], cn_r.at[0], other))]
+    xn = {}
     for i in range(1, nx):
-        to = lax.rem(x + i, nx)
-        p1.append(go(copy(pred_s.at[to], pall.at[zh, x], p1_s.at[i - 1], p1_r.at[i - 1], xdev(i, c))))
-    pall[zh, x] = pred_s[x]
-    pl.semaphore_wait(far, 2)
-    for cp in p1:
-        cp.wait_recv()
-    zorder = [nzh // 2] + [i for i in range(1, nzh) if i != nzh // 2]
-    p2 = {}
-    for i in zorder:
-        p2[i] = go(copy(pall.at[zh], pall.at[zh], p2_s.at[i - 1], p2_r.at[i - 1], zhdev(i)))
+        xn[i] = go(copy(norm_t.at[me], norm_t.at[me], xn_s.at[i - 1], xn_r.at[i - 1], xdev(i, c)))
     th = jnp.tanh(k0 * (v + k1 * v * v * v))
     gprime[...] = 0.5 * (1.0 + th) + 0.5 * v * (1.0 - th * th) * (k0 * (1.0 + 3.0 * k1 * v * v))
     pre[...] = 0.5 * v * (1.0 + th)
-    turn(pre, act_t)
-    ta = go(copy(act_t.at[c], act_t.at[c], tc_s.at[1], tc_r.at[1], other))
+    turn(pre, act_t.at[c])
+    ta = go(copy(act_t.at[c], act_t.at[c], tc_s.at[0], tc_r.at[0], other))
     for cp in lo_t:
         cp.wait()
     truth_s[...] = jnp.zeros_like(truth_s)
@@ -283,69 +298,70 @@
     cw_s[...] = jnp.zeros_like(cw_s)
     cw_s[pl.ds(0, 1), pl.ds(0, sz.chans)] = cw_r[...]
     weight = jnp.broadcast_to(cw_s[pl.ds(0, 1), :], (pad, pad)).T[:, 0:1] * area_r[...]
-    own = pred_s[...].reshape(pad, pts).astype(F32)
-    own = slope(own - truth_s[...])
-    mine = pall[zh].astype(F32)
-    pair = jnp.zeros((nx, quarter, pts), F32)
-    for i in [0] + zorder[1:] + zorder[:1]:
-        if i > 0:
-            p2[i].wait_recv()
-        src = lax.rem(zh - i + nzh, nzh)
-        for j in range(nx):
-            pair += slope(mine - pall[src, j].astype(F32)[None])
-    pair_s[...] = pair.astype(BF16)
-    p4 = []
-    for i in range(1, nx):
+    mine = pall[zh, x, send].astype(F32)
+    own = slope(mine - truth_s[send, :])
+    pair = jnp.zeros((sent_rows, pts), F32)
+
+    def add_pairs(total, i):
+        zs = lax.rem(zh - i + nzh, nzh)
+        total += slope(mine - pall[zs, x, send].astype(F32))
+        for j in xorder:
+            p2[i, j].wait_recv()
+            total += slope(mine - pall[zs, lax.rem(x - j + nx, nx), send].astype(F32))
+        return total
+
+    pair = add_pairs(pair, 0)
+    for i in zorder[1:]:
+        p1[i].wait_recv()
+        share(i)
+    for i in zorder[1:]:
+        pair = add_pairs(pair, i)
+    for k in range(1, nx):
+        xn[k].wait_recv()
+        got = norm_t.at[lax.rem(x - k + nx, nx) * 2 + c]
+        cn.append(go(copy(got, got, cn_s.at[k], cn_r.at[k], other)))
+    p1[zorder[0]].wait_recv()
+    share(zorder[0])
+    pair = add_pairs(pair, zorder[0])
+    pgrad = weight[0:sent_rows] * (own - pair / (nx * nzh - 1.0))
+    pg_o[...] = pgrad[0:sz.chans, :].reshape(sz.chans, 1, pts)
+    truth_s[send, :] = pgrad
+    if sent_rows < pad:
+        truth_s[pl.ds(sent_rows, pad - sent_rows), :] = jnp.zeros((pad - sent_rows, pts), F32)
+    gb[c] = truth_s[...].T.astype(BF16)
+    tg = go(copy(gb.at[c], gb.at[c], tc_s.at[1], tc_r.at[1], other))
+
+    for which in range(2):
+        w = wbuf[pl.ds(which * (nzl // 2), nzl // 2), :, :, :, pl.ds(hid, pad)].reshape(half, pad)
+        d_act = lax.dot_general(gb[c], w, NT, preferred_element_type=F32)
+        d_pre = (d_act * gprime[:, pl.ds(which * half, half)]).astype(BF16)
+        for xx in range(nx):
+            dp_send[which, xx] = d_pre[:, xx * tile:(xx + 1) * tile]
+    q1 = []
+    for i in xorder + [0]:
         to = lax.rem(x + i, nx)
-        p4.append(go(copy(pair_s.at[to], pair_r.at[x], p4_s.at[i - 1], p4_r.at[i - 1], xdev(i, c))))
-    pair_r[x] = pair_s[x]
-    for cp in p4:
-        cp.wait_recv()
-    pgrad = weight * (own - pair_r[...].astype(F32).reshape(pad, pts) / (nx * nzh - 1.0))
-    pg_o[...] = pgrad[0:sz.chans, :]
-    gb[c] = pgrad.T.astype(BF16)
-    tg = go(copy(gb.at[c], gb.at[c], tc_s.at[2], tc_r.at[2], other))
-
-    def d_pre(which):
-        zz = pl.ds(which * (nzl // 2), nzl // 2)
-        w = wbuf[zz, :, :, :, pl.ds(hid, pad)].reshape(half, pad)
-        d_act = lax.dot_general(gb[c], w, NT, preferred_element_type=F32)
-        return (d_act * gprime[:, pl.ds(pl.multiple_of(which * half, half), half)]).astype(BF16)
-
-    dp_send[...] = d_pre(oc)
-    td = go(copy(dp_send, dp_half.at[c], tc_s.at[3], tc_r.at[3], other))
-    dp_half[c] = d_pre(c)
-    tn.wait_recv()
-    td.wait_recv()
-
-    me_a, me_b = x + (y - x) * c, y + (x - y) * c
-    na = nx
-    def adev(i):
-        to = lax.rem(me_a + i, na)
-        return to, at(to + (x - to) * c, y + (to - y) * c, z, c)
-
-    def bdev(i):
-        to = lax.rem(me_b + i, na)
-        return to, at(x + (to - x) * c, to + (y - to) * c, z, c)
-
-    q1, q2 = {}, {}
+        for k, cc in ((0, c), (1, oc)):
+            if i > 0 or k > 0:
+                q1.append(go(copy(dp_send.at[cc, to], dp_all.at[me], q1_s.at[2 * i + k],
+                                  q1_r.at[2 * i + k], xdev(i, cc))))
+    dp_all[me] = dp_send[c, x]
+    for cp in cn:
+        cp.wait_recv()
+    for cp in q1:
+        cp.wait_recv()
+
+    q2 = {}
     for ch in range(nch):
-        def step(k, carry):
-            rows = pl.ds(pl.multiple_of((ch * zpc + k) * slab, slab), slab)
-            lhs = jnp.concatenate([norm_t[0, rows, :], norm_t[1, rows, :]], axis=1)
-            res = jnp.dot(lhs, dp_half[...].reshape(2 * pts, half), preferred_element_type=F32)
-            res = res.astype(BF16)
-            for yy in range(ny):
-                for xx in range(nx):
-                    a, b = xx + (yy - xx) * c, yy + (xx - yy) * c
-                    mb[ch, a, b, pl.ds(pl.multiple_of(k * two, two), two), :] = (
-                        res[yy * two:(yy + 1) * two, xx * tile:(xx + 1) * tile])
-            return carry
-        lax.fori_loop(0, zpc, step, 0)
-        for i in range(1, na):
-            to, dev = adev(i)
-            q1[ch, i] = go(copy(mb.at[ch, to], r1.at[ch, i - 1], q1_s.at[ch, i - 1],
-                                q1_r.at[ch, i - 1], dev))
+        rows = pl.ds(ch * zpc * slab, zpc * slab)
+        lhs = jnp.concatenate([norm_t[k, rows, :] for k in range(2 * nx)], axis=1)
+        res = jnp.dot(lhs, dp_all[...].reshape(2 * nx * pts, tile), preferred_element_type=F32)
+        res = res.astype(BF16).reshape(zpc, ny, two, tile)
+        for yy in range(ny):
+            mb[ch, yy] = res[:, yy]
+        for i in range(1, ny):
+            to = lax.rem(y + i, ny)
+            q2[ch, i] = go(copy(mb.at[ch, to], r2.at[ch, i - 1], q2_s.at[ch, i - 1],
+                                q2_r.at[ch, i - 1], ydev(i)))
 
     ta.wait_recv()
     tg.wait_recv()
@@ -366,18 +382,6 @@
         to = lax.rem(zl + d + nzl, nzl)
         u1.append(go(copy(ob.at[to], o1.at[j], u1_s.at[j], u1_r.at[j], zdev(d))))
 
-    for ch in range(nch):
-        for i in range(1, na):
-            q1[ch, i].wait_recv()
-        total = mb[ch, me_a].astype(F32)
-        for i in range(1, na):
-            total += r1[ch, i - 1].astype(F32)
-        s1[ch] = total
-        s2[ch] = total.astype(BF16)
-        for i in range(1, na):
-            to, dev = bdev(i)
-            q2[ch, i] = go(copy(s2.at[ch, to], r2.at[ch, i - 1], q2_s.at[ch, i - 1],
-                                q2_r.at[ch, i - 1], dev))
     for cp in u1:
         cp.wait_recv()
     total = obf[zl]
@@ -391,12 +395,11 @@
         u2.append(go(copy(o2s.at[to], o2.at[i - 1], u2_s.at[i - 1], u2_r.at[i - 1], ydev(i))))
     q3 = {}
     for ch in range(nch):
-        for i in range(1, na):
+        total = mb[ch, y].astype(F32)
+        for i in range(1, ny):
             q2[ch, i].wait_recv()
-        total = s1[ch, me_b]
-        for i in range(1, na):
             total += r2[ch, i - 1].astype(F32)
-        s3[pl.ds(ch * zpc, zpc)] = total.reshape(zpc, two, tile).astype(BF16)
+        s3[pl.ds(ch * zpc, zpc)] = total.astype(BF16)
         for zt in range(ch * zpc, (ch + 1) * zpc):
             d = lax.rem(zt - zl + 2 * nzl - 1 - nzl // 2, nzl) - (nzl // 2 - 1)
             q3[zt] = copy(s3.at[zt], r3.at[zl], q3_s.at[zt], q3_r.at[zl], zdev(d))
@@ -480,9 +483,7 @@
     half = hid // 2
     tile = half // nx
     pts, pad, nch = sz.points, sz.pad, sz.chunks
-    quarter = pad // nx
     zpc = nzl // nch
-    rc = zpc * 2 * ROWS
     win = max(nzl - 1, 1)
     V = pltpu.VMEM
 
@@ -501,25 +502,19 @@
         V((nzl, ny, 2, ROWS, hid + pad), BF16),
         V((2, sz.nodes, hid), BF16),
         V((pts, hid), BF16),
-        V((2, hid, pts), BF16),
+        V((2 * nx, hid, pts), BF16),
         V((2, hid, pts), BF16),
         V((pts, hid), F32),
         V((pts, hid), F32),
-        V((nx, quarter, pts), BF16),
         V((pad, pts), F32),
         V((8, pad), F32),
-        V((nzh, nx, quarter, pts), BF16),
-        V((nx, quarter, pts), BF16),
-        V((nx, quarter, pts), BF16),
+        V((nzh, nx, pad, pts), BF16),
         V((2, pts, pad), BF16),
-        V((pts, half), BF16),
-        V((2, pts, half), BF16),
+        V((2, nx, pts, tile), BF16),
+        V((2 * nx, pts, tile), BF16),
         V((ny, 2, ROWS, pad), F32),
-        V((nch, nx, ny, rc, tile), BF16),
-        V((nch, nx - 1, ny, rc, tile), BF16),
-        V((nch, ny, rc, tile), F32),
-        V((nch, ny, rc, tile), BF16),
-        V((nch, ny - 1, rc, tile), BF16),
+        V((nch, ny, zpc, 2 * ROWS, tile), BF16),
+        V((nch, ny - 1, zpc, 2 * ROWS, tile), BF16),
         V((nzl, 2 * ROWS, tile), BF16),
         V((nzl, 2 * ROWS, tile), BF16),
         V((nzl, ny, ROWS, pad), BF16),
@@ -536,9 +531,10 @@
         pltpu.SemaphoreType.REGULAR,
         pltpu.SemaphoreType.DMA((9,)),
     ]
-    scratch += sems(nzl) + sems(nzl, ny - 1) + sems(nx - 1) + sems(nzl) + sems(2) + sems(4)
-    scratch += sems(nx - 1) + sems(nzh - 1) + sems(nx - 1)
-    scratch += sems(nch, nx - 1) + sems(nch, ny - 1) + sems(nzl) + sems(nzh - 1)
+    scratch += sems(nx - 1) + sems(nx)
+    scratch += sems(nzl) + sems(nzl, ny - 1) + sems(nx - 1, ny) + sems(nzl) + sems(2) + sems(2)
+    scratch += sems(nzh - 1) + sems(nzh, nx - 1)
+    scratch += sems(2 * nx) + sems(nch, ny - 1) + sems(nzl) + sems(nzh - 1)
     scratch += sems(2 * nx - 1) + sems(nx - 1) + sems(win) + sems(ny - 1)
     vmem = pl.BlockSpec(memory_space=pltpu.VMEM)
     outs = pl.pallas_call(
@@ -547,7 +543,7 @@
             jax.ShapeDtypeStruct((ROWS, hid), F32),
             jax.ShapeDtypeStruct((ROWS, sz.chans), F32),
             jax.ShapeDtypeStruct((1, ROWS), F32),
-            jax.ShapeDtypeStruct((sz.chans, pts), F32),
+            jax.ShapeDtypeStruct((sz.chans, 1, pts), F32),
         ),
         in_specs=[pl.BlockSpec(memory_space=pltpu.HBM)] * 9,
         out_specs=(vmem,) * 4,
@@ -558,7 +554,7 @@
     )(*[pltpu.with_memory_space_constraint(a, pltpu.HBM) for a in (
         mesh_latent[0], grid_latent[0], edges.T, truth, area[None], chan_weight[None], gain[None],
         w_hidden, w_out)])
-    return outs[0], outs[1], outs[2][0], outs[3][None]
+    return outs[0], outs[1], outs[2][0], outs[3].transpose(1, 0, 2)
 
 
 def program(mesh, sz):

time: 112 us -> 106 us (0.946)
  Pallas kernels: 109 us -> 102 us
    pallas_call x1, Pallas kernels: 109 us -> 102 us  [body(): pl.pallas_call(functools.partial(kernel, sz), out_shape=(jax.ShapeDtypeSt...]
where the time goes in v3:
time: 106 us; the launch traced here: 105 us
  Pallas kernels  102 us (96%)
  local copies, waits for them, and re-layouts  2.36 us (2%)
    pallas_call x1, Pallas kernels, body(): pl.pallas_call(functools.partial(kernel, sz), out_shape=(jax.ShapeDtypeSt...  102 us
    unnamed x4, local copies, waits for them, and re-layouts  2.36 us

profile of v3, /device:TPU:1, one launch (start us, length us, event | category | flops | bytes accessed | tf_op | source)
XLA Modules:
  0.0 105.5 jit_solution(16305359517660829501)
XLA Ops:
  0.6 102.5 %shard_map.120 = (f32[16,1024]{1,0:T(8,128)S(1)}, f32[16,100]{1,0:T(8,128)S(1)}, f32[1,16]{1,0:T(1,128)S(1)}, f32[100,1,128]{2,1,0:T(1,128)S(1)}) custom-call(bf16[64,1024]{1,0:T(8,128)(2,1)} %bitcast.11, bf16[128,1024]{1,0:T(8,128)(2,1)} %bitcast.10, s32[3,128]{1,0:T(4,128)} %bitcast.13, f32[100,128]{1,0:T(8,128)} %truth_h.1, f32[1,128]{1,0:T(1,128)} %bitcast.14, ...), custom_call_target="tpu_custom_call" | custom-call | flops 1000000000 | bytes 1000000 | tf_op jit(solution)/shard_map/pallas_call | solution.py:540
  103.1 0.6 copy.17
  103.7 0.6 copy.18
  104.3 0.5 copy.19
  104.8 0.6 copy.20

commit v4 on v3

--- a/solution.py
+++ b/solution.py
@@ -73,6 +73,8 @@
             window.append(-d)
     window = window[: nzl - 1]
 
+    sg = 1 - 2 * c
+
     def zdev(d):
         return at(x, y, lax.rem(z + d + nz, nz), c)
 
@@ -140,7 +142,7 @@
     signal(near, zdev(-reach))
 
     block = wbuf.at[zl, y, c]
-    wz = {d: copy(block, block, wz_s.at[j], wz_r.at[zl], zdev(d)) for j, d in enumerate(window)}
+    wz = {d: copy(block, block, wz_s.at[j], wz_r.at[zl], zdev(sg * d)) for j, d in enumerate(window)}
 
     @pl.when(spread)
     def _():
@@ -162,7 +164,7 @@
 
     evens = [0] + [-d for d in window if d % 2 == 0]
     odds = [-d for d in window if d % 2 == 1]
-    za = [lax.rem(zl + e + (o - e) * odd + nzl, nzl) for e, o in zip(evens, odds, strict=True)]
+    za = [lax.rem(zl + sg * (e + (o - e) * odd) + nzl, nzl) for e, o in zip(evens, odds, strict=True)]
     nk = len(za)
     wy = {}
 
@@ -379,8 +381,8 @@
     lax.fori_loop(0, nzl, out_step, 0)
     u1 = []
     for j, d in enumerate(window):
-        to = lax.rem(zl + d + nzl, nzl)
-        u1.append(go(copy(ob.at[to], o1.at[j], u1_s.at[j], u1_r.at[j], zdev(d))))
+        to = lax.rem(zl + sg * d + nzl, nzl)
+        u1.append(go(copy(ob.at[to], o1.at[j], u1_s.at[j], u1_r.at[j], zdev(sg * d))))
 
     for cp in u1:
         cp.wait_recv()
@@ -401,8 +403,8 @@
             total += r2[ch, i - 1].astype(F32)
         s3[pl.ds(ch * zpc, zpc)] = total.astype(BF16)
         for zt in range(ch * zpc, (ch + 1) * zpc):
-            d = lax.rem(zt - zl + 2 * nzl - 1 - nzl // 2, nzl) - (nzl // 2 - 1)
-            q3[zt] = copy(s3.at[zt], r3.at[zl], q3_s.at[zt], q3_r.at[zl], zdev(d))
+            d = lax.rem(sg * (zt - zl) + 2 * nzl - 1 - nzl // 2, nzl) - (nzl // 2 - 1)
+            q3[zt] = copy(s3.at[zt], r3.at[zl], q3_s.at[zt], q3_r.at[zl], zdev(sg * d))
 
             @pl.when(zl != zt)
             def _(zt=zt):

time: 106 us -> 107 us (level)
  no operation moved by 1% of the time
where the time goes in v4:
time: 107 us; the launch traced here: 106 us
  Pallas kernels  103 us (96%)
  local copies, waits for them, and re-layouts  2.36 us (2%)
    pallas_call x1, Pallas kernels, body(): pl.pallas_call(functools.partial(kernel, sz), out_shape=(jax.ShapeDtypeSt...  103 us
    unnamed x4, local copies, waits for them, and re-layouts  2.36 us

profile of v4, /device:TPU:1, one launch (start us, length us, event | category | flops | bytes accessed | tf_op | source)
XLA Modules:
  0.0 106.5 jit_solution(13903474339375743662)
XLA Ops:
  0.6 103.5 %shard_map.120 = (f32[16,1024]{1,0:T(8,128)S(1)}, f32[16,100]{1,0:T(8,128)S(1)}, f32[1,16]{1,0:T(1,128)S(1)}, f32[100,1,128]{2,1,0:T(1,128)S(1)}) custom-call(bf16[64,1024]{1,0:T(8,128)(2,1)} %bitcast.11, bf16[128,1024]{1,0:T(8,128)(2,1)} %bitcast.10, s32[3,128]{1,0:T(4,128)} %bitcast.13, f32[100,128]{1,0:T(8,128)} %truth_h.1, f32[1,128]{1,0:T(1,128)} %bitcast.14, ...), custom_call_target="tpu_custom_call" | custom-call | flops 1000000000 | bytes 1000000 | tf_op jit(solution)/shard_map/pallas_call | solution.py:542
  104.1 0.6 copy.17
  104.7 0.6 copy.18
  105.3 0.5 copy.19
  105.8 0.6 copy.20
